TPU v7x, 256 devices: a whole 4x4x8 slice. The times are simulated.
256 devices in a mesh: master: 8 (over x, core), region: 32 (over z, y).
Axes of the slice: x: 4, y: 4, z: 8, core: 2. Of those that a mesh axis runs over, the one named last changes fastest.
Arguments:
- masters: float32 [1024, 128, 128], P('master'), may hold values from 0 to 1
- inst_master: int32 [8, 32, 16], P(None, 'region'), may hold values from 0 to 127
- inst_row: int32 [8, 32, 16], P(None, 'region'), may hold values from 0 to 256
- inst_col: int32 [8, 32, 16], P(None, 'region'), may hold values from 0 to 896
- def_index: int32 [32], P('region'), may hold values from 0 to 7
- def_weights: float32 [8, 12], replicated, may hold values from 0.1 to 1
- kernels: bfloat16 [24, 225], replicated, may hold values from -0.375 to 0.375
- target: bfloat16 [32, 384, 1024], P('region', 'master'), may hold values from 0 to 1
Outputs:
- master_grad: float32 [1024, 128, 128], P('master')
- resist: bfloat16 [32, 384, 1024], P('region', 'master')
Inputs may be any that keep to these rules, and one draw needn't show every extreme that they name: inst_master[s, r, i] names master s * 128 + inst_master[s, r, i], an instance in the tile of region r; panels of one tile may intersect. `inst_row`: every placed panel lies wholly inside its tile. `inst_col`: every placed panel lies wholly inside its tile.
All inputs are finite; a program needn't handle non-finite values.
Results may differ from a plain program's by a relative error of at most 0.0061.
Values may be sent and summed in bfloat16 or wider, within the bound.
No kernel may reach another device: no remote copies, remote signals or barrier semaphores. Data moves between devices by JAX's collectives and lax.ppermute only.
A program may use at most 128 MiB of HBM per device.

v0:
```python
import jax
import jax.numpy as jnp
from jax import lax
from jax.sharding import PartitionSpec as P

TC = 1024
TR = 48
KS = 15
KERN = 12
P_SIZE = 128
MAS_DEV = 128
INST_DEV = 16


STEEP = 1.5
THRESH = 3.0


def extended_2(x, sides, width):
    for axis, dim in sides:
        peers, length = (lax.axis_size(axis), x.shape[dim])
        up = [(i, (i + 1) % peers) for i in range(peers - 1)]
        down = [(j, i) for i, j in up]
        last = lax.slice_in_dim(x, length - width, length, axis=dim)
        first = lax.slice_in_dim(x, 0, width, axis=dim)
        before = lax.ppermute(last, axis, up)
        after = lax.ppermute(first, axis, down)
        x = jnp.concatenate([before, x, after], axis=dim)
    return x


def toeplitz_table(kernels, flipped):
    kernel_grid = kernels.astype(jnp.float32).reshape(2 * KERN, KS, KS)
    if flipped:
        kernel_grid = kernel_grid[:, ::-1, ::-1]
    window_width = 128 + KS - 1
    offset = jnp.arange(window_width)[:, None] - jnp.arange(128)[None, :]
    select = (offset[None, :, :] == jnp.arange(KS)[:, None, None]).astype(jnp.float32)
    toeplitz = jnp.einsum("cab,bwt->awct", kernel_grid, select, precision=lax.Precision.HIGHEST)
    return toeplitz.astype(jnp.bfloat16)


def column_windows(field):
    margin = (KS - 1) // 2
    pad_spec = [(0, 0)] * (field.ndim - 1) + [(margin, 128 - margin)]
    padded = jnp.pad(field, pad_spec)
    blocked = padded.reshape(field.shape[:-1] + (field.shape[-1] // 128 + 1, 128))
    return jnp.concatenate([blocked[..., :-1, :], blocked[..., 1:, : KS - 1]], axis=-1)


def place_panels(canvas, panels, row_at, col_at, weight):

    def add_one(slot_index, current):
        corner = (row_at[slot_index], col_at[slot_index])
        patch_sum = lax.dynamic_slice(current, corner, (P_SIZE, P_SIZE)) + weight[
            slot_index
        ] * panels[slot_index].astype(jnp.float32)
        return lax.dynamic_update_slice(current, patch_sum, corner)

    return lax.fori_loop(0, panels.shape[0], add_one, canvas)


def body(masters, inst_master, inst_row, inst_col, def_index, def_weights, kernels, target):
    shard_count = lax.axis_size("master")
    shard_index = lax.axis_index("master")
    margin = (KS - 1) // 2
    rim_width = KS - 1
    tile_rows = TR * shard_count
    band_start = shard_index * TR
    ext_rows = TR + rim_width
    block_count = TC // 128
    panel_values = masters.astype(jnp.bfloat16)
    all_ids = inst_master[:, 0, :]
    all_rows = inst_row[:, 0, :]
    all_cols = inst_col[:, 0, :]
    own_ids = lax.dynamic_index_in_dim(all_ids, shard_index, 0, keepdims=False)
    own_rows = lax.dynamic_index_in_dim(all_rows, shard_index, 0, keepdims=False)
    own_cols = lax.dynamic_index_in_dim(all_cols, shard_index, 0, keepdims=False)
    own_panels = jnp.take(panel_values, own_ids, axis=0)
    target_band = target[0]
    canvas = jnp.zeros((tile_rows, TC), jnp.float32)
    layout = place_panels(
        canvas, own_panels, own_rows, own_cols, jnp.ones((INST_DEV,), jnp.float32)
    )
    band_mask = lax.psum_scatter(layout, "master", scatter_dimension=0, tiled=True).astype(
        jnp.bfloat16
    )
    stacked = jnp.stack([band_mask, target_band])
    extended = extended_2(stacked, (("master", 1),), rim_width)
    mask_ext = extended[0]
    target_ext = extended[1, margin : margin + ext_rows]
    forward_table = toeplitz_table(kernels, False)
    mask_windows = column_windows(mask_ext)
    tap_rows = jnp.stack(
        [mask_windows[tap_index : tap_index + ext_rows] for tap_index in range(KS)], axis=2
    )
    fields = jnp.einsum(
        "yjaw,awct->ycjt", tap_rows, forward_table, preferred_element_type=jnp.float32
    )
    fields = fields.reshape(ext_rows, 2 * KERN, TC)
    level_pick = (jnp.arange(def_weights.shape[0]) == def_index[0]).astype(jnp.float32)
    focus_weights = jnp.sum(level_pick[:, None] * def_weights, axis=0)
    doubled = jnp.concatenate([focus_weights, focus_weights])
    intensity = jnp.sum(doubled[None, :, None] * fields * fields, axis=1)
    resist_level = 1.0 / (1.0 + jnp.exp(-STEEP * (intensity - THRESH)))
    global_row = band_start - margin + jnp.arange(ext_rows)
    inside = ((global_row >= 0) & (global_row < tile_rows)).astype(jnp.float32)
    slope_term = (
        STEEP
        * (resist_level - target_ext.astype(jnp.float32))
        * resist_level
        * (1.0 - resist_level)
        * inside[:, None]
    )
    cotangent = (2.0 * doubled[None, :, None] * slope_term[:, None, :] * fields).astype(
        jnp.bfloat16
    )
    resist = resist_level[margin : margin + TR].astype(jnp.bfloat16)[None]
    adjoint_table = toeplitz_table(kernels, True)
    cot_windows = column_windows(cotangent)

    def add_tap(tap_index, running):
        rows_part = lax.dynamic_slice_in_dim(cot_windows, tap_index, TR, 0)
        taps_part = lax.dynamic_index_in_dim(adjoint_table, tap_index, 0, keepdims=False)
        return running + jnp.einsum(
            "ycjw,wct->yjt", rows_part, taps_part, preferred_element_type=jnp.float32
        )

    mask_grad = lax.fori_loop(
        0, KS, add_tap, jnp.zeros((TR, block_count, 128), jnp.float32)
    ).reshape(TR, TC)
    full_grad = lax.all_gather(mask_grad, "master", axis=0, tiled=True)

    def cut_block(row_first, col_first):
        return lax.dynamic_slice(full_grad, (row_first, col_first), (P_SIZE, P_SIZE))

    pieces = jax.vmap(cut_block)(own_rows, own_cols)
    owner_pick = (own_ids[None, :] == jnp.arange(MAS_DEV)[:, None]).astype(jnp.float32)
    summed = jnp.einsum("mi,ipq->mpq", owner_pick, pieces, precision=lax.Precision.HIGHEST)
    master_grad = lax.psum(summed, "region")
    return (master_grad, resist)


def solution(mesh):
    return jax.shard_map(
        body,
        mesh=mesh,
        in_specs=(
            P("master", None, None),
            P(None, "region", None),
            P(None, "region", None),
            P(None, "region", None),
            P("region"),
            P(),
            P(),
            P("region", "master", None),
        ),
        out_specs=(P("master", None, None), P("region", "master", None)),
        check_vma=False,
    )
```

profile of v0, /device:TPU:6, one launch (start us, length us, event | category | flops | bytes accessed | tf_op | source)
XLA Modules:
  0.0 639.4 jit_solution(2191569195495538252)
XLA Ops:
  8.5 6.4 convert_element_type.68
  14.9 2.9 gather_fusion
  18.8 114.0 %while.28 = (s32[]{:T(128)}, f32[384,1024]{1,0:T(8,128)S(1)}, s32[16]{0:T(128)S(1)}, s32[16]{0:T(128)S(1)}, bf16[16,128,128]{2,1,0:T(8,128)(2,1)S(1)}, /*index=5*/s32[]{:T(128)}, s32[]{:T(128)}, s32[]{:T(128)}, s32[]{:T(128)}) while((s32[]{:T(128)}, f32[384,1024]{1,0:T(8,128)S(1)}, s32[16]{0:T(128)S(1)}, s32[16]{0:T(128)S(1)}, ...), condition=%wide.region_2.3_spmd, body=%wide.region_1.2_spmd.sunk | while | flops 32776 | bytes 295113 | solution.py:60
  24.0 2.0 dynamic_update_slice.8
  31.2 2.0 dynamic_update_slice.8
  38.5 2.0 dynamic_update_slice.8
  45.7 2.0 dynamic_update_slice.8
  59.9 1.9 dynamic_update_slice.8
  73.9 2.0 dynamic_update_slice.8
  95.0 2.0 dynamic_update_slice.8
  102.3 2.0 dynamic_update_slice.8
  109.5 2.0 dynamic_update_slice.8
  123.6 1.9 dynamic_update_slice.8
  130.7 2.0 dynamic_update_slice.8
  135.5 6.7 %convert_bitcast_fusion.1 = bf16[15,142,24,128,1]{3,2,0,1,4:T(8,128)(2,1)} fusion(s32[142,128]{1,0:T(8,128)S(1)} %iota_subtract_fusion, bf16[24,15,15]{0,2,1:T(8,128)(2,1)S(1)} %copy.96), kind=kOutput, calls=%fused_computation.13 | convolution fusion | flops 203116800 | bytes 13170224 | tf_op jit(solution)/shard_map/cab,bwt->awct/dot_general | solution.py:39
  142.3 13.3 %convert_bitcast_fusion = bf16[15,142,24,128]{3,2,0,1:T(8,128)(2,1)} fusion(s32[142,128]{1,0:T(8,128)S(1)} %iota_subtract_fusion, f32[24,15,15]{0,2,1:T(8,128)S(1)} %copy.116), kind=kOutput, calls=%fused_computation.12 | convolution fusion | flops 1184620800 | bytes 13181024 | tf_op jit(solution)/shard_map/cab,bwt->awct/dot_general | solution.py:39
  155.5 14.2 %reduce-scatter.2.cloned.1.call-done = f32[48,1024]{1,0:T(8,128)} async-done(((f32[384,1024]{1,0:T(8,128)}), f32[48,1024]{1,0:T(8,128)}) %reduce-scatter.2.cloned.1.call-update) | async-done | bytes 196624 | tf_op jit(solution)/shard_map/reduce_scatter | solution.py:85
  170.7 3.5 collective-permute-start
  174.2 2.1 collective-permute-start.1
  179.7 10.6 %fusion.11 = (f32[62,8,128]{2,0,1:T(8,128)S(1)}, f32[62,24,8,128]{3,0,2,1:T(8,128)S(1)}) fusion(f32[24]{0:T(128)S(1)} %get-tuple-element.263, bf16[62,8,15,142]{3,0,2,1:T(8,128)(2,1)S(1)} %fusion.23, bf16[15,142,24,128,1]{3,2,0,1,4:T(8,128)(2,1)} %convert_bitcast_fusion.1), kind=kOutput, calls=%fused_computation.15 | convolution fusion | flops 6495520768 | bytes 21548576 | tf_op jit(solution)/shard_map/yjaw,awct->ycjt/dot_general | solution.py:97
  190.6 6.2 copy.115
  196.8 7.1 %reshape.208 = f32[62,24,1024]{2,1,0:T(8,128)} reshape(f32[62,24,8,128]{3,2,1,0:T(8,128)} %copy.115) | data formatting | bytes 12189696 | tf_op jit(solution)/shard_map/reshape | solution.py:100
  203.9 3.8 multiply_convert_fusion
  207.8 2.0 pad.9
  209.8 4.2 reshape.209
  214.0 2.7 copy-done
  218.6 4.3 pad_maximum_fusion
  222.9 80.1 %while.30 = (s32[]{:T(128)}, f32[48,8,128]{2,1,0:T(8,128)S(1)}, bf16[62,24,8,142]{3,2,1,0:T(8,128)(2,1)}, bf16[15,142,24,128]{3,2,0,1:T(8,128)(2,1)}, s32[]{:T(128)}, /*index=5*/s32[]{:T(128)}) while((s32[]{:T(128)}, f32[48,8,128]{2,1,0:T(8,128)S(1)}, bf16[62,24,8,142]{3,2,1,0:T(8,128)(2,1)}, bf16[15,142,24,128]{3,2,0,1:T(8,128)(2,1)}, ...), condition=%wide.region_6.7_spmd.clone, body=%wide.region_5.6_spmd.clone.sunk | while | flops 335118336 | bytes 7729747 | solution.py:129
  224.2 4.0 fusion.65
  229.6 4.0 fusion.65
  234.9 4.0 fusion.65
  240.2 4.0 fusion.65
  245.6 4.0 fusion.65
  250.9 4.0 fusion.65
  256.3 4.0 fusion.65
  261.6 4.0 fusion.65
  267.0 4.0 fusion.65
  272.3 4.0 fusion.65
  277.7 4.0 fusion.65
  283.0 4.0 fusion.65
  288.3 4.0 fusion.65
  293.7 4.0 fusion.65
  299.0 4.0 fusion.65
  304.5 27.1 %all-gather.2.cloned.1.call-done = f32[384,1024]{1,0:T(8,128)} async-done(((f32[48,1024]{1,0:T(8,128)}), f32[384,1024]{1,0:T(8,128)}) %all-gather.2.cloned.1.call-update) | async-done | bytes 1572880 | tf_op jit(solution)/shard_map/all_gather | solution.py:132
  331.6 70.1 %while.29 = (s32[]{:T(128)}, f32[384,1024]{1,0:T(8,128)}, s32[16,2]{0,1:T(2,128)S(1)}, f32[16,128,128]{2,0,1:T(8,128)S(1)}, s32[]{:T(128)}, /*index=5*/s32[]{:T(128)}) while((s32[]{:T(128)}, f32[384,1024]{1,0:T(8,128)}, s32[16,2]{0,1:T(2,128)S(1)}, f32[16,128,128]{2,0,1:T(8,128)S(1)}, s32[]{:T(128)}, /*index=5*/s32[]{:T(128)}) %tuple.95), condition=%wide.while_cond, body=%wide.while_body.sunk | while | flops 2 | bytes 262257 | solution.py:135
  332.2 2.3 dynamic-slice.10
  336.6 2.3 dynamic-slice.10
  341.0 2.3 dynamic-slice.10
  345.4 2.3 dynamic-slice.10
  349.8 2.3 dynamic-slice.10
  354.1 2.3 dynamic-slice.10
  358.5 2.3 dynamic-slice.10
  362.9 2.3 dynamic-slice.10
  367.3 2.3 dynamic-slice.10
  371.7 2.3 dynamic-slice.10
  376.1 2.3 dynamic-slice.10
  380.4 2.3 dynamic-slice.10
  384.8 2.3 dynamic-slice.10
  389.2 2.3 dynamic-slice.10
  393.6 2.3 dynamic-slice.10
  398.0 2.3 dynamic-slice.10
  401.7 5.8 fusion.50
  409.2 212.0 %all-reduce.4.cloned.1.call-done = f32[128,128,128]{2,0,1:T(8,128)} async-done(((f32[128,128,128]{2,0,1:T(8,128)}), f32[128,128,128]{2,0,1:T(8,128)}) %all-reduce.4.cloned.1.call-update) | async-done | bytes 8388624 | tf_op jit(solution)/shard_map/psum | solution.py:140
  621.2 11.6 %copy.119 = f32[128,128,128]{2,1,0:T(8,128)} copy(f32[128,128,128]{2,0,1:T(8,128)} %all-reduce.4.cloned.1.call-done) | data formatting | bytes 16777216
  (190 shorter events, 96.5 us)
Async XLA Ops:
  7.2 162.6 %reduce-scatter.2.cloned.1.call-start = ((), (), s32[]{:S(2)}) async-start(), calls=%async_computation.1 | async-start | bytes 1769472 | tf_op jit(solution)/shard_map/reduce_scatter | solution.py:85
  14.9 119.1 %copy-start.5 = (bf16[24,225]{1,0:T(8,128)(2,1)S(1)}, bf16[24,225]{1,0:T(8,128)(2,1)}, u32[]{:S(2)}) copy-start(bf16[24,225]{1,0:T(8,128)(2,1)} %param.18) | copy-start | bytes 32404
  14.9 120.4 %copy-start.6 = (f32[8,12]{1,0:T(8,128)S(1)}, f32[8,12]{1,0:T(8,128)}, u32[]{:S(2)}) copy-start(f32[8,12]{1,0:T(8,128)} %param.17) | copy-start | bytes 1156
  132.8 1.1 copy-start.1
  134.0 197.6 %all-gather.2.cloned.1.call-start = ((), (), s32[]{:S(2)}) async-start(), calls=%async_computation.2 | async-start | bytes 1769472 | tf_op jit(solution)/shard_map/all_gather | solution.py:132
  142.2 28.4 %copy-start.4 = (bf16[1,48,1024]{2,1,0:T(8,128)(2,1)S(1)}, bf16[1,48,1024]{2,1,0:T(8,128)(2,1)}, u32[]{:S(2)}) copy-start(bf16[1,48,1024]{2,1,0:T(8,128)(2,1)} %param.19) | copy-start | bytes 294916
  170.7 5.6 collective-permute-start
  174.2 4.0 collective-permute-start.1
  190.6 13.3 %copy-start.3 = (f32[8,8,8,128]{3,1,2,0:T(8,128)}, f32[8,8,8,128]{3,1,2,0:T(8,128)S(1)}, u32[]{:S(2)}) copy-start(f32[8,8,8,128]{3,1,2,0:T(8,128)S(1)} %copy.133) | copy-start | bytes 786436
  214.0 2.7 copy-start
  216.7 1.9 slice-start
  218.6 4.3 copy-start.2
  303.8 317.4 %all-reduce.4.cloned.1.call-start = ((), (), s32[]{:S(2)}) async-start(), calls=%async_computation.3 | async-start | bytes 16777216 | tf_op jit(solution)/shard_map/psum | solution.py:140
Sparse Core Ops, SparseCore 0:
  134.1 35.6 reduce-scatter.1
  303.9 27.6 all-gather.1
  407.7 213.4 all-reduce.3
where the time goes:
time: 644 us; the launch traced here: 639 us
  waiting for transfers between devices  255 us (40%)
  local copies, waits for them, and re-layouts  184 us (29%)
  matrix products  96 us (15%)
  loops' own time  63.5 us (10%)
  other arithmetic  19.8 us (3%)
  between operations  14.8 us (2%)
    psum x1, waiting for transfers between devices, body(): master_grad = lax.psum(summed, 'region')  212 us
    gather x64, local copies, waits for them, and re-layouts  69.7 us
    another operation x1, loops' own time, place_panels(): return lax.fori_loop(0, panels.shape[0], add_one, canvas)  62.7 us
    dot_general x15, matrix products, add_tap(): jnp.einsum('ycjw,wct->yjt', rows_part, taps_part, preferred_element_type=...  59.6 us
    dynamic_update_slice x16, local copies, waits for them, and re-layouts, add_one(): return lax.dynamic_update_slice(current, patch_sum, corner)  30.9 us
    all_gather x1, waiting for transfers between devices, body(): full_grad = lax.all_gather(mask_grad, 'master', axis=0, tiled=True)  27.1 us
    dynamic_slice x15, local copies, waits for them, and re-layouts, add_tap(): lax.dynamic_index_in_dim(adjoint_table, tap_index, 0, keepdims=False)  20.1 us
    dot_general x2, matrix products, toeplitz_table(): jnp.einsum('cab,bwt->awct', kernel_grid, select, precision=lax.Precision....  20 us
  transfers between devices with their start and end apart: 5, of which 4 were waited for; matrix products, arithmetic and copies ran while one was open for 4% of the time, Pallas kernels for 0%

commit v1 on v0

v1 whole, which is shorter than its diff:
```python
import functools
import jax, jax.numpy as jnp
from jax import lax
from jax.experimental import pallas as pl
from jax.sharding import PartitionSpec as P
from jax.experimental.pallas import tpu as pltpu

TC = 1024; TR = 48; KS = 15; KERN = 12; P_SIZE = 128; MAS_DEV = 128; INST_DEV = 16
STEEP = 1.5; THRESH = 3.0
BR, BC = 8, 16
H = 7
ROWB = 8
MROWB = ROWB + 2
COLB = TC // BC
M = ROWB * COLB
K = 6 * 128
F32, BF = jnp.float32, jnp.bfloat16


def swap_chunks(x):
    n = x.shape[0]
    row = lax.broadcasted_iota(jnp.int32, (n, 128), 0)
    chunk = lax.broadcasted_iota(jnp.int32, (n, 128), 1) // BC

    def sub(v, k):
        return pltpu.roll(v.reshape(n // 8, 8, 128), k, 1).reshape(n, 128)

    for k in (1, 2, 4):
        rbit = (row & k) != 0
        cbit = (chunk & k) != 0
        up = sub(pltpu.roll(x, 128 - BC * k, 1), k)
        if k == 4:
            dn = up
        else:
            dn = sub(pltpu.roll(x, BC * k, 1), 8 - k)
        x = jnp.where(rbit == cbit, x, jnp.where(rbit, up, dn))
    return x


def to_blocks(x):
    a, b = x.shape[0] // 8, x.shape[1] // 128
    tiles = [x[8 * i : 8 * i + 8, 128 * t : 128 * t + 128] for i in range(a) for t in range(b)]
    return swap_chunks(jnp.concatenate(tiles, axis=0))


def from_blocks(v, a, b):
    x = swap_chunks(v)
    rows = []
    for i in range(a):
        rows.append(jnp.concatenate([x[(i * b + t) * 8 : (i * b + t) * 8 + 8] for t in range(b)], axis=1))
    return jnp.concatenate(rows, axis=0)


def table_kernel(v_ref, w_ref):
    lane = lax.broadcasted_iota(jnp.int32, (16, 512), 1) % BC
    row = lax.broadcasted_iota(jnp.int32, (16, 512), 0)
    low = lane <= row

    def one(c, carry):
        x = jnp.broadcast_to(v_ref[c], (16, 512))
        r = pltpu.roll(x, 1, 1, stride=1, stride_axis=0)
        lo = jnp.where(low, r, 0.0)
        hi = jnp.where(low, 0.0, r)
        for p in range(8):
            lp = (pltpu.roll(lo, 512 - 16 * p, 1) if p else lo).astype(BF)
            hp = (pltpu.roll(hi, 512 - 16 * p, 1) if p else hi).astype(BF)
            for wy in range(24):
                dy, yw = wy // 8, wy % 8
                if (24 - wy) % 8 == p:
                    q = (24 - wy) // 8
                    w_ref[c, (dy * 2) * 128 + yw * 16 : (dy * 2) * 128 + yw * 16 + 16, :] = lp[:, 128 * q : 128 * q + 128]
                if (23 - wy) % 8 == p:
                    q = (23 - wy) // 8
                    w_ref[c, (dy * 2 + 1) * 128 + yw * 16 : (dy * 2 + 1) * 128 + yw * 16 + 16, :] = hp[:, 128 * q : 128 * q + 128]
        return carry

    lax.fori_loop(0, 2 * KERN, one, 0)


def taps_rows(kernels):
    k = kernels.astype(F32).reshape(2 * KERN, KS, KS)
    k = k[:, ::-1, ::-1]
    k = jnp.pad(k, ((0, 0), (9, 32 - 9 - KS), (1, 0)))
    return k.reshape(2 * KERN, 1, 512)


def make_table(kernels):
    return pl.pallas_call(
        table_kernel,
        out_shape=jax.ShapeDtypeStruct((2 * KERN, K, 128), BF),
        in_specs=[pl.BlockSpec(memory_space=pltpu.VMEM)],
        out_specs=pl.BlockSpec(memory_space=pltpu.VMEM),
        compiler_params=pltpu.CompilerParams(vmem_limit_bytes=32 * 1024 * 1024),
        name="taps_table",
    )(taps_rows(kernels))


def image_kernel(level_ref, shard_ref, wgt_ref, above_ref, mid_ref, below_ref, tabove_ref, tmid_ref, tbelow_ref, w_ref,
                 resist_ref, grad_ref, lhs_ref, fields_ref, cot_ref):
    level_at = level_ref[0]
    x = jnp.concatenate([above_ref[...].astype(F32), mid_ref[...].astype(BF).astype(F32), below_ref[...].astype(F32)], axis=0)
    x = pltpu.roll(x, 8 * MROWB - 1, 0)
    x = jnp.concatenate([x, jnp.zeros((8 * MROWB, 128), F32)], axis=1)
    x = pltpu.roll(x, H, 1)
    mb = to_blocks(x).reshape(MROWB, 72, 128)
    for dy in range(3):
        for dx in range(2):
            part = mb[dy : dy + ROWB, dx : dx + COLB, :]
            lhs_ref[:, (dy * 2 + dx) * 128 : (dy * 2 + dx) * 128 + 128] = part.reshape(M, 128).astype(BF)
    intensity = jnp.zeros((M, 128), F32)
    for c in range(KERN):
        acc = None
        for part in range(2):
            f = jnp.dot(lhs_ref[...], w_ref[part * KERN + c], preferred_element_type=F32)
            fields_ref[part * KERN + c] = f
            acc = f * f if acc is None else acc + f * f
        intensity = intensity + wgt_ref[level_at, c] * acc
    level = 1.0 / (1.0 + jnp.exp(-STEEP * (intensity - THRESH)))
    resist_ref[...] = from_blocks(level, ROWB, 8)[8 : 8 + TR].astype(BF)
    goal = jnp.concatenate([tabove_ref[...].astype(F32)[8:], tmid_ref[...].astype(F32), tbelow_ref[...].astype(F32)[:8]], axis=0)
    goal = to_blocks(goal)
    slope = STEEP * (level - goal) * level * (1.0 - level)
    row_block = lax.broadcasted_iota(jnp.int32, (M, 128), 0) // COLB
    in_block = lax.broadcasted_iota(jnp.int32, (M, 128), 1) // BC
    at = shard_ref[0] * TR - 8 + row_block * 8 + in_block
    slope = jnp.where((at >= 0) & (at < 8 * TR), slope, 0.0)
    for c in range(KERN):
        s = 2.0 * wgt_ref[level_at, c] * slope
        for part in range(2):
            i = part * KERN + c
            cot_ref[:, i * 128 : i * 128 + 128] = (s * fields_ref[i]).astype(BF)
    out = [None] * 7
    for dy in range(3):
        for dx in range(2):
            q = dy * 2 + dx
            acc = jnp.zeros((M, 128), F32)
            for c in range(2 * KERN):
                acc = acc + lax.dot_general(cot_ref[:, c * 128 : c * 128 + 128], w_ref[c, q * 128 : q * 128 + 128, :],
                                            (((1,), (1,)), ((), ())), preferred_element_type=F32)
            for i in range(ROWB):
                j = i + dy
                if 1 <= j <= 7:
                    piece = acc[i * COLB : i * COLB + COLB]
                    z8 = jnp.zeros((8, 128), F32)
                    piece = jnp.concatenate([piece, z8], axis=0)
                    if dx:
                        piece = pltpu.roll(piece, 1, 0)
                    out[j - 1] = piece if out[j - 1] is None else out[j - 1] + piece
    nat = from_blocks(jnp.concatenate(out, axis=0), 7, 9)
    nat = pltpu.roll(nat, 9 * 128 - H, 1)
    grad_ref[...] = nat[H : H + TR, :TC].astype(grad_ref.dtype)


def image(level, shard, weights, above, mid, below, tabove, tmid, tbelow, table):
    vm = pl.BlockSpec(memory_space=pltpu.VMEM)
    sm = pl.BlockSpec(memory_space=pltpu.SMEM)
    return pl.pallas_call(
        image_kernel,
        out_shape=(jax.ShapeDtypeStruct((TR, TC), BF), jax.ShapeDtypeStruct((TR, TC), BF)),
        in_specs=[sm] * 3 + [vm] * 7,
        out_specs=(vm, vm),
        scratch_shapes=[pltpu.VMEM((M, K), BF), pltpu.VMEM((2 * KERN, M, 128), F32), pltpu.VMEM((M, 2 * KERN * 128), BF)],
        compiler_params=pltpu.CompilerParams(vmem_limit_bytes=48 * 1024 * 1024),
        name="image",
    )(level, shard, weights, above, mid, below, tabove, tmid, tbelow, table)


def own(shard_ref, *refs):
    s = shard_ref[0]
    return [[ref[s, 0, i] for i in range(INST_DEV)] for ref in refs]


WIDE = TC + 128
LEAD = 16

def place_kernel(shard_ref, ids_ref, rows_ref, cols_ref, masters_ref, out_ref, panels, canvas, sem):
    ids, rows, cols = own(shard_ref, ids_ref, rows_ref, cols_ref)
    copies = []
    for i in range(INST_DEV):
        cp = pltpu.make_async_copy(masters_ref.at[ids[i]], panels.at[i], sem.at[i])
        cp.start()
        copies.append(cp)
    canvas[...] = jnp.zeros(canvas.shape, F32)
    lane = lax.broadcasted_iota(jnp.int32, (P_SIZE, 128), 1)
    for i in range(INST_DEV):
        copies[i].wait()
        p = panels[i].astype(BF).astype(F32)
        c = cols[i]
        c0 = (c // 128) * 128
        d = c - c0
        p = pltpu.roll(p, d, 1)
        left = jnp.where(lane >= d, p, 0.0)
        right = jnp.where(lane >= d, 0.0, p)
        full = jnp.concatenate([jnp.concatenate([left, right], axis=1), jnp.zeros((8, 256), F32)], axis=0)
        r = rows[i] + LEAD
        r0 = (r // 8) * 8
        full = pltpu.roll(full, r - r0, 0)
        at = (pl.ds(pl.multiple_of(r0, 8), P_SIZE + 8), pl.ds(pl.multiple_of(c0, 128), 256))
        canvas[at] = canvas[at] + full
    out_ref[...] = canvas[LEAD : LEAD + 8 * TR, :TC].reshape(8, TR, TC).astype(out_ref.dtype)


def place(shard, ids, rows, cols, masters):
    return pl.pallas_call(
        place_kernel,
        out_shape=jax.ShapeDtypeStruct((8, TR, TC), F32),
        in_specs=[pl.BlockSpec(memory_space=pltpu.SMEM)] * 4 + [pl.BlockSpec(memory_space=pl.ANY)],
        out_specs=pl.BlockSpec(memory_space=pltpu.VMEM),
        scratch_shapes=[pltpu.VMEM((INST_DEV, P_SIZE, P_SIZE), F32), pltpu.VMEM((LEAD + 8 * TR + 16, WIDE), F32), pltpu.SemaphoreType.DMA((INST_DEV,))],
        compiler_params=pltpu.CompilerParams(vmem_limit_bytes=32 * 1024 * 1024),
        name="place",
    )(shard, ids, rows, cols, masters)


def cut_kernel(shard_ref, ids_ref, rows_ref, cols_ref, grad_ref, out_ref, canvas, sums):
    ids, rows, cols = own(shard_ref, ids_ref, rows_ref, cols_ref)
    canvas[: 8 * TR, :TC] = grad_ref[...].astype(F32)
    lane = lax.broadcasted_iota(jnp.int32, (P_SIZE, 128), 1)
    out_ref[...] = jnp.zeros(out_ref.shape, out_ref.dtype)
    sums[...] = jnp.zeros(sums.shape, F32)
    slots = []
    for i in range(INST_DEV):
        c = cols[i]
        c0 = (c // 128) * 128
        d = c - c0
        r = rows[i]
        r0 = (r // 8) * 8
        full = canvas[pl.ds(pl.multiple_of(r0, 8), P_SIZE + 8), pl.ds(pl.multiple_of(c0, 128), 256)]
        full = pltpu.roll(full, P_SIZE + 8 - (r - r0), 0)[:P_SIZE]
        full = pltpu.roll(full, 256 - d, 1)[:, :128]
        slot = jnp.int32(i)
        for j in range(i - 1, -1, -1):
            slot = jnp.where(ids[j] == ids[i], jnp.int32(j), slot)
        slots.append(slot)
        sums[slot] = sums[slot] + full
    for i in range(INST_DEV):
        out_ref[ids[i]] = sums[slots[i]].astype(out_ref.dtype)


def cut(shard, ids, rows, cols, grad):
    vm = pl.BlockSpec(memory_space=pltpu.VMEM)
    return pl.pallas_call(
        cut_kernel,
        out_shape=jax.ShapeDtypeStruct((MAS_DEV, P_SIZE, P_SIZE), BF),
        in_specs=[pl.BlockSpec(memory_space=pltpu.SMEM)] * 4 + [vm],
        out_specs=vm,
        scratch_shapes=[pltpu.VMEM((8 * TR + 8, WIDE), F32), pltpu.VMEM((INST_DEV, P_SIZE, P_SIZE), F32)],
        compiler_params=pltpu.CompilerParams(vmem_limit_bytes=32 * 1024 * 1024),
        name="cut",
    )(shard, ids, rows, cols, grad)


def halo(x, axis, width):
    n = lax.axis_size(axis)
    above = lax.ppermute(x[-width:], axis, [(i, i + 1) for i in range(n - 1)])
    below = lax.ppermute(x[:width], axis, [(i + 1, i) for i in range(n - 1)])
    return above, below


def body(masters, inst_master, inst_row, inst_col, def_index, def_weights, kernels, target):
    shard = lax.axis_index("master").reshape(1)
    tmid = target[0]
    tabove, tbelow = halo(tmid, "master", 16)
    layout = place(shard, inst_master, inst_row, inst_col, masters)
    mid = lax.psum_scatter(layout.reshape(8 * TR, TC), "master", scatter_dimension=0, tiled=True)
    table = make_table(kernels)
    above, below = halo(mid.astype(BF), "master", 16)
    resist, grad = image(def_index, shard, def_weights, above, mid, below, tabove, tmid, tbelow, table)
    full = lax.all_gather(grad, "master", axis=0, tiled=True)
    summed = cut(shard, inst_master, inst_row, inst_col, full)
    master_grad = lax.psum(summed.astype(F32), "region")
    return (master_grad, resist[None])


def solution(mesh):
    return jax.shard_map(
        body,
        mesh=mesh,
        in_specs=(
            P("master", None, None),
            P(None, "region", None),
            P(None, "region", None),
            P(None, "region", None),
            P("region"),
            P(),
            P(),
            P("region", "master", None),
        ),
        out_specs=(P("master", None, None), P("region", "master", None)),
        check_vma=False,
    )
```

time: 644 us -> 301 us (0.47)
  waiting for transfers between devices: 255 us -> 30.7 us
  blocking collectives: 0 us -> 210 us
  local copies, waits for them, and re-layouts: 184 us -> 8.13 us
  matrix products: 96 us -> 0 us
  loops' own time: 63.5 us -> 0 us
  Pallas kernels: 0 us -> 25.3 us
  other arithmetic: 19.8 us -> 1.01 us
    psum x1 -> x0, waiting for transfers between devices: 212 us -> none  [body(): master_grad = lax.psum(summed, 'region')]
    psum x0 -> x1, blocking collectives: none -> 196 us  [body(): master_grad = lax.psum(summed.astype(F32), 'region')]
    dot_general x19 -> x0, matrix products: 96 us -> none  [the longest x15 59.6 us: add_tap(): jnp.einsum('ycjw,wct->yjt', rows_part, taps_part, preferred_element_type=...]
    gather x65 -> x0, local copies, waits for them, and re-layouts: 72.5 us -> none
    another operation x3 -> x0, loops' own time: 63.5 us -> none  [the longest x1 62.7 us: place_panels(): return lax.fori_loop(0, panels.shape[0], add_one, canvas)]
    dynamic_slice x47 -> x0, local copies, waits for them, and re-layouts: 38.9 us -> none  [the longest x15 20.1 us: add_tap(): lax.dynamic_index_in_dim(adjoint_table, tap_index, 0, keepdims=False)]
    dynamic_update_slice x16 -> x0, local copies, waits for them, and re-layouts: 30.9 us -> none  [add_one(): return lax.dynamic_update_slice(current, patch_sum, corner)]
    all_gather x1 -> x0, waiting for transfers between devices: 27.1 us -> none  [body(): full_grad = lax.all_gather(mask_grad, 'master', axis=0, tiled=True)]
  transfers between devices with their start and end apart: 5 -> 5, of which waited for: 4 -> 1; matrix products, arithmetic and copies ran while one was open for 4% -> 1% of each run, Pallas kernels for 0% -> 2%
where the time goes in v1:
time: 301 us; the launch traced here: 299 us
  blocking collectives  210 us (70%)
  waiting for transfers between devices  30.7 us (10%)
  Pallas kernels  25.3 us (8%)
  between operations  14.9 us (5%)
  starting transfers between devices  9.24 us (3%)
  local copies, waits for them, and re-layouts  8.13 us (3%)
    psum x1, blocking collectives, body(): master_grad = lax.psum(summed.astype(F32), 'region')  196 us
    reduce_scatter x1, waiting for transfers between devices, body(): lax.psum_scatter(layout.reshape(8 * TR, TC), 'master', scatter_dimension=...  30.7 us
    all_gather x1, blocking collectives, body(): full = lax.all_gather(grad, 'master', axis=0, tiled=True)  13.8 us
    pallas_call x1, Pallas kernels, image(): pl.pallas_call(image_kernel, out_shape=(jax.ShapeDtypeStruct((TR, TC), BF...  12.5 us
    unnamed x24, local copies, waits for them, and re-layouts  7.43 us
  transfers between devices with their start and end apart: 5, of which 1 were waited for; matrix products, arithmetic and copies ran while one was open for 1% of the time, Pallas kernels for 2%

profile of v1, /device:TPU:6, one launch (start us, length us, event | category | flops | bytes accessed | tf_op | source)
XLA Modules:
  0.0 299.4 jit_solution(4788025644308600460)
XLA Ops:
  7.2 0.0 reduce-scatter.2.cloned.1.call-start
  7.2 0.0 copy-start.1
  7.2 3.4 %copy-done.1 = f32[128,128,128]{2,1,0:T(8,128)S(1)} copy-done((f32[128,128,128]{2,1,0:T(8,128)S(1)}, f32[128,128,128]{2,1,0:T(8,128)}, u32[]{:S(2)}) %copy-start.1) | copy-done | bytes 8388632
  10.6 0.0 copy-start.4
  10.6 0.7 copy-done.4
  11.3 0.0 copy-start.6
  11.3 0.7 copy-done.6
  12.0 0.0 copy-start.8
  12.0 0.7 copy-done.8
  12.7 0.0 copy-start.3
  12.7 0.0 copy-start.11
  12.7 5.6 %place.1 = f32[8,48,1024]{2,1,0:T(8,128)} custom-call(s32[1]{0:T(128)} %bitcast.shard_ref, s32[8,1,16]{2,1,0:T(1,128)S(1)} %copy-done.4, s32[8,1,16]{2,1,0:T(1,128)S(1)} %copy-done.6, s32[8,1,16]{2,1,0:T(1,128)S(1)} %copy-done.8, f32[128,128,128]{2,1,0:T(8,128)S(1)} %copy-done.1), custom_call_target="tpu_custom_call" | custom-call | tf_op jit(solution)/shard_map/place/pallas_call | solution.py:204
  18.3 0.0 copy-start.10
  18.3 0.0 reduce-scatter.2.cloned.1.call-update
  18.4 0.0 copy-done.3
  18.4 2.2 collective-permute-start.3
  20.6 2.1 collective-permute-start.2
  22.7 30.7 %reduce-scatter.2.cloned.1.call-done.mid_ref = f32[48,1024]{1,0:T(8,128)} async-done(((f32[384,1024]{1,0:T(8,128)}), f32[48,1024]{1,0:T(8,128)}) %reduce-scatter.2.cloned.1.call-update) | async-done | bytes 196624 | tf_op jit(solution)/shard_map/reduce_scatter | solution.py:265
  53.4 0.0 copy-start.2
  53.4 1.0 convert_element_type.9
  54.5 1.9 collective-permute-start.1
  56.4 3.0 collective-permute-start
  60.0 0.0 copy-done.11
  60.0 0.1 reshape.27
  60.1 0.2 rev.3
  60.4 0.1 pad.4
  60.5 0.2 reshape.28.v_ref
  60.7 0.0 copy-start.5
  60.7 0.0 copy-start.7
  60.7 0.0 copy-start.9
  60.8 4.9 %taps_table.1.w_ref = bf16[24,768,128]{2,1,0:T(8,128)(2,1)S(1)} custom-call(f32[24,1,512]{2,1,0:T(1,128)S(1)} %reshape.28.v_ref), custom_call_target="tpu_custom_call" | custom-call | tf_op jit(solution)/shard_map/taps_table/pallas_call | solution.py:88
  65.7 0.0 collective-permute-done.3.tbelow_ref
  65.7 0.0 collective-permute-done.2.tabove_ref
  65.7 0.0 collective-permute-done.1.below_ref
  65.7 0.0 collective-permute-done.above_ref
  65.7 0.0 copy-done.10
  65.7 0.0 copy-done.2
  65.7 12.5 %image.1 = (bf16[48,1024]{1,0:T(8,128)(2,1)}, bf16[48,1024]{1,0:T(8,128)(2,1)S(1)}) custom-call(s32[1]{0:T(128)S(6)} %copy.13.level_ref, s32[1]{0:T(128)} %bitcast.shard_ref, f32[8,12]{1,0:T(8,128)S(1)} %copy-done.10, bf16[16,1024]{1,0:T(8,128)(2,1)S(1)} %collective-permute-done.above_ref, f32[48,1024]{1,0:T(8,128)S(1)} %copy-done.2, ...), custom_call_target="tpu_custom_call" | custom-call | tf_op jit(solution)/shard_map/image/pallas_call | solution.py:157
  78.2 13.8 %all_gather.3.grad_ref = bf16[384,1024]{1,0:T(8,128)(2,1)S(1)} all-gather(bf16[48,1024]{1,0:T(8,128)(2,1)S(1)} %get-tuple-element.4), channel_id=1, replica_groups=mesh['master'=8,'region'=32] {'master'}, dimensions={0}, use_global_device_ids=true | all-gather | bytes 884736 | tf_op jit(solution)/shard_map/all_gather | solution.py:269
  92.1 0.0 copy-done.5
  92.1 0.0 copy-done.7
  92.1 0.0 copy-done.9
  92.1 2.2 cut.1
  94.3 0.0 copy-start
  94.3 2.0 copy-done
  96.2 196.3 %all-reduce.2 = f32[128,128,128]{2,1,0:T(8,128)} all-reduce(bf16[128,128,128]{2,1,0:T(8,128)(2,1)} %copy-done), channel_id=1, replica_groups=mesh['master'=8,'region'=32] {'region'}, use_global_device_ids=true, to_apply=%region_1.2 | all-reduce | flops 2097152 | bytes 12582912 | tf_op jit(solution)/shard_map/psum | solution.py:271
  (2 shorter events, 0.0 us)
Async XLA Ops:
  7.2 46.3 %reduce-scatter.2.cloned.1.call-start = ((), (), s32[]{:S(2)}) async-start(), calls=%async_computation.1 | async-start | bytes 1769472 | tf_op jit(solution)/shard_map/reduce_scatter | solution.py:265
  7.2 3.4 %copy-start.1 = (f32[128,128,128]{2,1,0:T(8,128)S(1)}, f32[128,128,128]{2,1,0:T(8,128)}, u32[]{:S(2)}) copy-start(f32[128,128,128]{2,1,0:T(8,128)} %masters_ref.1) | copy-start | bytes 25165828
  10.6 0.7 copy-start.4
  11.3 0.7 copy-start.6
  12.0 0.7 copy-start.8
  12.7 5.7 %copy-start.3 = (bf16[1,48,1024]{2,1,0:T(8,128)(2,1)S(1)}, bf16[1,48,1024]{2,1,0:T(8,128)(2,1)}, u32[]{:S(2)}) copy-start(bf16[1,48,1024]{2,1,0:T(8,128)(2,1)} %param.15) | copy-start | bytes 294916
  12.7 47.3 %copy-start.11 = (bf16[24,225]{1,0:T(8,128)(2,1)S(1)}, bf16[24,225]{1,0:T(8,128)(2,1)}, u32[]{:S(2)}) copy-start(bf16[24,225]{1,0:T(8,128)(2,1)} %param.14) | copy-start | bytes 32404
  18.3 47.4 %copy-start.10 = (f32[8,12]{1,0:T(8,128)S(1)}, f32[8,12]{1,0:T(8,128)}, u32[]{:S(2)}) copy-start(f32[8,12]{1,0:T(8,128)} %wgt_ref.1) | copy-start | bytes 1156
  18.4 47.3 %collective-permute-start.3 = (bf16[16,1024]{1,0:T(8,128)(2,1)S(1)}, bf16[16,1024]{1,0:T(8,128)(2,1)S(1)}, u32[]{:S(2)}, u32[]{:S(2)}) collective-permute-start(bf16[16,1024]{1,0:T(8,128)(2,1)S(1)} %get-tuple-element.6), channel_id=1, source_target_pairs={{32,0},{64,32},{96,64},{128,96},{160,128},{192,160},{224,192},{33,... | collective-permute-start | bytes 98312 | tf_op jit(solution)/shard_map/ppermute | solution.py:256
  20.6 45.1 %collective-permute-start.2 = (bf16[16,1024]{1,0:T(8,128)(2,1)S(1)}, bf16[16,1024]{1,0:T(8,128)(2,1)S(1)}, u32[]{:S(2)}, u32[]{:S(2)}) collective-permute-start(bf16[16,1024]{1,0:T(8,128)(2,1)S(1)} %get-tuple-element.7), channel_id=1, source_target_pairs={{0,32},{32,64},{64,96},{96,128},{128,160},{160,192},{192,224},{1,3... | collective-permute-start | bytes 98312 | tf_op jit(solution)/shard_map/ppermute | solution.py:255
  53.4 12.3 %copy-start.2 = (f32[48,1024]{1,0:T(8,128)S(1)}, f32[48,1024]{1,0:T(8,128)}, u32[]{:S(2)}) copy-start(f32[48,1024]{1,0:T(8,128)} %reduce-scatter.2.cloned.1.call-done.mid_ref) | copy-start | bytes 589828
  54.5 11.2 %collective-permute-start.1 = (bf16[16,1024]{1,0:T(8,128)(2,1)S(1)}, bf16[16,1024]{1,0:T(8,128)(2,1)S(1)}, u32[]{:S(2)}, u32[]{:S(2)}) collective-permute-start(bf16[16,1024]{1,0:T(8,128)(2,1)S(1)} %get-tuple-element.8), channel_id=1, source_target_pairs={{32,0},{64,32},{96,64},{128,96},{160,128},{192,160},{224,192},{33,... | collective-permute-start | bytes 98312 | tf_op jit(solution)/shard_map/ppermute | solution.py:256
  56.4 9.3 %collective-permute-start = (bf16[16,1024]{1,0:T(8,128)(2,1)S(1)}, bf16[16,1024]{1,0:T(8,128)(2,1)S(1)}, u32[]{:S(2)}, u32[]{:S(2)}) collective-permute-start(bf16[16,1024]{1,0:T(8,128)(2,1)S(1)} %get-tuple-element.9), channel_id=1, source_target_pairs={{0,32},{32,64},{64,96},{96,128},{128,160},{160,192},{192,224},{1,3... | collective-permute-start | bytes 98312 | tf_op jit(solution)/shard_map/ppermute | solution.py:255
  60.7 31.4 %copy-start.5 = (s32[8,1,16]{2,1,0:T(1,128)S(1)}, s32[8,1,16]{2,1,0:T(1,128)}, u32[]{:S(2)}) copy-start(s32[8,1,16]{2,1,0:T(1,128)} %ids_ref.3) | copy-start | bytes 1540
  60.7 31.4 %copy-start.7 = (s32[8,1,16]{2,1,0:T(1,128)S(1)}, s32[8,1,16]{2,1,0:T(1,128)}, u32[]{:S(2)}) copy-start(s32[8,1,16]{2,1,0:T(1,128)} %rows_ref.3) | copy-start | bytes 1540
  60.7 31.3 %copy-start.9 = (s32[8,1,16]{2,1,0:T(1,128)S(1)}, s32[8,1,16]{2,1,0:T(1,128)}, u32[]{:S(2)}) copy-start(s32[8,1,16]{2,1,0:T(1,128)} %cols_ref.3) | copy-start | bytes 1540
  94.3 2.0 copy-start
Sparse Core Ops, SparseCore 0:
  18.5 34.9 reduce-scatter.1
